TPU v7x, 32 devices: a whole 2x2x4 slice. The times are simulated.
32 devices in a mesh: dp: 8 (over z, x), tensor: 4 (over y, core).
Axes of the slice: x: 2, y: 2, z: 4, core: 2. Of those that a mesh axis runs over, the one named last changes fastest.
Arguments:
- inputs: bfloat16 [8192, 768], P(('dp', 'tensor')), may hold values from -6 to 6
- cotangent: bfloat16 [8192, 768], P(('dp', 'tensor')), may hold values from -6 to 6
- qkv_weight: bfloat16 [3, 768, 768], P(None, 'dp', 'tensor'), may hold values from -0.21582031 to 0.21582031
- proj_weight: bfloat16 [768, 768], P('tensor', 'dp'), may hold values from -3.453125 to 3.453125
- up_weight: bfloat16 [768, 3072], P('dp', 'tensor'), may hold values from -0.21875 to 0.21875
- down_weight: bfloat16 [3072, 768], P('tensor', 'dp'), may hold values from -0.109375 to 0.109375
- qv_bias: bfloat16 [2, 768], P(None, ('tensor', 'dp')), may hold values from -3 to 3
- up_bias: bfloat16 [3072], P(('tensor', 'dp')), may hold values from -3 to 3
- norm_gains: bfloat16 [2, 768], P(None, ('dp', 'tensor')), may hold values from 0.5 to 1.5
- row_biases: bfloat16 [4, 768], P(None, ('dp', 'tensor')), may hold values from -3 to 3
Outputs:
- outputs: bfloat16 [8192, 768], P(('dp', 'tensor'))
- input_grad: float32 [8192, 768], P(('dp', 'tensor'))
- qkv_grad: float32 [3, 768, 768], P(None, 'dp', 'tensor')
- proj_grad: float32 [768, 768], P('tensor', 'dp')
- up_grad: float32 [768, 3072], P('dp', 'tensor')
- down_grad: float32 [3072, 768], P('tensor', 'dp')
- qv_bias_grad: float32 [2, 768], P(None, ('tensor', 'dp'))
- up_bias_grad: float32 [3072], P(('tensor', 'dp'))
- gains_grad: float32 [2, 768], P(None, ('dp', 'tensor'))
- biases_grad: float32 [4, 768], P(None, ('dp', 'tensor'))
All inputs are finite; a program needn't handle non-finite values.
Results may differ from a plain program's by a relative error of at most 0.018.
The roundings to bfloat16 on the way count: a program that leaves them out, or rounds other values in their place, can miss the bound.
Values may be sent and summed in bfloat16 or wider, within the bound.
A program may use at most 128 MiB of HBM per device.

v0:
```python
import jax
import jax.numpy as jnp
from jax import lax
from jax.sharding import PartitionSpec as P

HD = 64


EPSILON = 1e-05
SCALE = 0.125
ROOT_HALF = 0.7071067811865476
ROOT_TWO_PI_INVERSE = 0.3989422804014327


def layer_norm(values, gain_row, shift_row):
    center = values - jnp.mean(values, axis=-1, keepdims=True)
    spread = jnp.mean(center * center, axis=-1, keepdims=True)
    return center * lax.rsqrt(spread + EPSILON) * gain_row + shift_row


def norm_back(values, gain_row, incoming):
    center = values - jnp.mean(values, axis=-1, keepdims=True)
    spread = jnp.mean(center * center, axis=-1, keepdims=True)
    inverse = lax.rsqrt(spread + EPSILON)
    unit_rows = center * inverse
    scaled = incoming * gain_row
    grad_in = inverse * (
        scaled
        - jnp.mean(scaled, axis=-1, keepdims=True)
        - unit_rows * jnp.mean(scaled * unit_rows, axis=-1, keepdims=True)
    )
    return (grad_in, jnp.sum(incoming * unit_rows, axis=0), jnp.sum(incoming, axis=0))


def gelu_exact(values):
    return 0.5 * values * (1.0 + jax.scipy.special.erf(values * ROOT_HALF))


def gelu_slope(values):
    cumulative = 0.5 * (1.0 + jax.scipy.special.erf(values * ROOT_HALF))
    return cumulative + values * jnp.exp(-0.5 * values * values) * ROOT_TWO_PI_INVERSE


def spread_frames(piece):
    return lax.all_gather(piece, "tensor", axis=0, tiled=True)


def reduce_frames(partial_sum):
    return lax.psum_scatter(
        partial_sum.astype(jnp.bfloat16), "tensor", scatter_dimension=0, tiled=True
    ).astype(jnp.float32)


def fetch_attention(qkv_weight, proj_weight, qv_bias):
    return (
        lax.all_gather(qkv_weight, "dp", axis=1, tiled=True),
        lax.all_gather(proj_weight, "dp", axis=1, tiled=True),
        lax.all_gather(qv_bias, "dp", axis=1, tiled=True),
    )


def fetch_mlp(up_weight, down_weight, up_bias):
    return (
        lax.all_gather(up_weight, "dp", axis=0, tiled=True),
        lax.all_gather(down_weight, "dp", axis=1, tiled=True),
        lax.all_gather(up_bias, "dp", axis=0, tiled=True),
    )


def head_forward(queries, key_rows, value_rows, block_rows):
    block_count = queries.shape[0] // block_rows

    def one_block(query_block):
        scores = (
            jnp.einsum("qe,ke->qk", query_block, key_rows, preferred_element_type=jnp.float32)
            * SCALE
        )
        row_max = jnp.max(scores, axis=1, keepdims=True)
        exponent = jnp.exp(scores - row_max)
        row_total = jnp.sum(exponent, axis=1, keepdims=True)
        probs_low = (exponent / row_total).astype(jnp.bfloat16)
        mixture = jnp.dot(probs_low, value_rows, preferred_element_type=jnp.float32)
        return (mixture, (row_max + jnp.log(row_total))[:, 0])

    mixture, logsum = lax.map(one_block, queries.reshape(block_count, block_rows, queries.shape[1]))
    return (mixture.reshape(queries.shape), logsum.reshape(queries.shape[0]))


def head_backward(queries, key_rows, value_rows, logsum, grad_mixed, block_rows):
    block_count = queries.shape[0] // block_rows
    width = queries.shape[1]

    def one_block(running, pieces):
        key_grad, value_grad = running
        query_block, logsum_block, grad_block = pieces
        scores = (
            jnp.einsum("qe,ke->qk", query_block, key_rows, preferred_element_type=jnp.float32)
            * SCALE
        )
        attn_probs = jnp.exp(scores - logsum_block[:, None])
        prob_grad = jnp.einsum(
            "qe,ke->qk", grad_block, value_rows, preferred_element_type=jnp.float32
        )
        row_dot = jnp.sum(attn_probs * prob_grad, axis=1, keepdims=True)
        score_grad = (attn_probs * (prob_grad - row_dot)).astype(jnp.bfloat16)
        query_grad = jnp.dot(score_grad, key_rows, preferred_element_type=jnp.float32) * SCALE
        key_grad = (
            key_grad
            + jnp.einsum("qk,qe->ke", score_grad, query_block, preferred_element_type=jnp.float32)
            * SCALE
        )
        value_grad = value_grad + jnp.einsum(
            "qk,qe->ke",
            attn_probs.astype(jnp.bfloat16),
            grad_block,
            preferred_element_type=jnp.float32,
        )
        return ((key_grad, value_grad), query_grad.astype(jnp.bfloat16))

    zeros_kv = jnp.zeros(key_rows.shape, jnp.float32)
    (key_grad, value_grad), query_grad = lax.scan(
        one_block,
        (zeros_kv, zeros_kv),
        (
            queries.reshape(block_count, block_rows, width),
            logsum.reshape(block_count, block_rows),
            grad_mixed.reshape(block_count, block_rows, width),
        ),
    )
    return (
        query_grad.reshape(queries.shape),
        key_grad.astype(jnp.bfloat16),
        value_grad.astype(jnp.bfloat16),
    )


def body(
    inputs,
    cotangent,
    qkv_weight,
    proj_weight,
    up_weight,
    down_weight,
    qv_bias,
    up_bias,
    norm_gains,
    row_biases,
):
    gains_full, biases_full = (
        lax.all_gather(norm_gains, ("dp", "tensor"), axis=1, tiled=True),
        lax.all_gather(row_biases, ("dp", "tensor"), axis=1, tiled=True),
    )
    gains_full = gains_full.astype(jnp.float32)
    biases_full = biases_full.astype(jnp.float32)
    frames_local = inputs.astype(jnp.float32)
    total_frames = inputs.shape[0] * lax.axis_size("tensor")
    block_rows = min(512, total_frames)
    qkv_full, proj_full, qv_full = fetch_attention(qkv_weight, proj_weight, qv_bias)
    local_heads = qkv_full.shape[2] // HD

    def split_heads(matrix):
        return matrix.reshape(total_frames, local_heads, HD).transpose(1, 0, 2)

    def join_heads(stacked):
        return stacked.transpose(1, 0, 2).reshape(total_frames, local_heads * HD)

    normed = spread_frames(
        layer_norm(frames_local, gains_full[0], biases_full[0]).astype(jnp.bfloat16)
    )
    projected = jnp.einsum("td,cde->cte", normed, qkv_full, preferred_element_type=jnp.float32)
    bias_float = qv_full.astype(jnp.float32)
    head_q = split_heads((projected[0] + bias_float[0]).astype(jnp.bfloat16))
    head_k = split_heads(projected[1].astype(jnp.bfloat16))
    head_v = split_heads((projected[2] + bias_float[1]).astype(jnp.bfloat16))

    def forward_head(triple):
        return head_forward(triple[0], triple[1], triple[2], block_rows)

    mixture, logsum = lax.map(forward_head, (head_q, head_k, head_v))
    attended = join_heads(mixture).astype(jnp.bfloat16)
    branch = reduce_frames(jnp.dot(attended, proj_full, preferred_element_type=jnp.float32))
    middle = frames_local + branch + biases_full[1]
    up_full, down_full, up_bias_full = fetch_mlp(up_weight, down_weight, up_bias)
    grad_out = cotangent.astype(jnp.float32)
    feed_bias_grad = jnp.sum(grad_out, axis=0)
    normed_two = spread_frames(
        layer_norm(middle, gains_full[1], biases_full[2]).astype(jnp.bfloat16)
    )
    hidden = jnp.dot(normed_two, up_full, preferred_element_type=jnp.float32) + up_bias_full.astype(
        jnp.float32
    )
    activated = gelu_exact(hidden).astype(jnp.bfloat16)
    feed_sum = reduce_frames(jnp.dot(activated, down_full, preferred_element_type=jnp.float32))
    outputs = (middle + feed_sum + biases_full[3]).astype(jnp.bfloat16)
    grad_full = spread_frames(cotangent)
    up_back, down_back = (up_full, down_full)
    down_grad = jnp.einsum("tf,td->fd", activated, grad_full, preferred_element_type=jnp.float32)
    act_grad = jnp.einsum("td,fd->tf", grad_full, down_back, preferred_element_type=jnp.float32)
    hidden_grad = (act_grad * gelu_slope(hidden)).astype(jnp.bfloat16)
    up_bias_grad = jnp.sum(hidden_grad.astype(jnp.float32), axis=0)
    up_grad = jnp.einsum("td,tf->df", normed_two, hidden_grad, preferred_element_type=jnp.float32)
    normed_two_grad = reduce_frames(
        jnp.einsum("tf,df->td", hidden_grad, up_back, preferred_element_type=jnp.float32)
    )
    middle_part, gain_two_grad, shift_two_grad = norm_back(middle, gains_full[1], normed_two_grad)
    middle_grad = grad_out + middle_part
    up_grad_out, down_grad_out, up_bias_out = (
        lax.psum_scatter(up_grad, "dp", scatter_dimension=0, tiled=True),
        lax.psum_scatter(down_grad, "dp", scatter_dimension=1, tiled=True),
        lax.psum_scatter(up_bias_grad, "dp", scatter_dimension=0, tiled=True),
    )
    proj_bias_grad = jnp.sum(middle_grad, axis=0)
    attn_grad_full = spread_frames(middle_grad.astype(jnp.bfloat16))
    qkv_back, proj_back = (qkv_full, proj_full)
    proj_grad = jnp.einsum(
        "te,td->ed", attended, attn_grad_full, preferred_element_type=jnp.float32
    )
    attended_grad = jnp.einsum(
        "td,ed->te", attn_grad_full, proj_back, preferred_element_type=jnp.float32
    ).astype(jnp.bfloat16)

    def backward_head(pieces):
        return head_backward(pieces[0], pieces[1], pieces[2], pieces[3], pieces[4], block_rows)

    head_dq, head_dk, head_dv = lax.map(
        backward_head, (head_q, head_k, head_v, logsum, split_heads(attended_grad))
    )
    query_grad = join_heads(head_dq)
    key_grad = join_heads(head_dk)
    value_grad = join_heads(head_dv)
    stacked_grads = jnp.stack([query_grad, key_grad, value_grad])
    qkv_grad = jnp.einsum("td,cte->cde", normed, stacked_grads, preferred_element_type=jnp.float32)
    qv_bias_grad = jnp.stack(
        [
            jnp.sum(query_grad.astype(jnp.float32), axis=0),
            jnp.sum(value_grad.astype(jnp.float32), axis=0),
        ]
    )
    normed_grad = reduce_frames(
        jnp.einsum("cte,cde->td", stacked_grads, qkv_back, preferred_element_type=jnp.float32)
    )
    input_part, gain_one_grad, shift_one_grad = norm_back(frames_local, gains_full[0], normed_grad)
    input_grad = middle_grad + input_part
    qkv_grad_out, proj_grad_out, qv_bias_out = (
        lax.psum_scatter(qkv_grad, "dp", scatter_dimension=1, tiled=True),
        lax.psum_scatter(proj_grad, "dp", scatter_dimension=1, tiled=True),
        lax.psum_scatter(qv_bias_grad, "dp", scatter_dimension=1, tiled=True),
    )
    gains_grad = jnp.stack([gain_one_grad, gain_two_grad])
    biases_grad = jnp.stack([shift_one_grad, proj_bias_grad, shift_two_grad, feed_bias_grad])
    gains_out, biases_out = (
        lax.psum_scatter(gains_grad, ("dp", "tensor"), scatter_dimension=1, tiled=True),
        lax.psum_scatter(biases_grad, ("dp", "tensor"), scatter_dimension=1, tiled=True),
    )
    return (
        outputs,
        input_grad,
        qkv_grad_out,
        proj_grad_out,
        up_grad_out,
        down_grad_out,
        qv_bias_out,
        up_bias_out,
        gains_out,
        biases_out,
    )


def solution(mesh):
    placed = (
        P(("dp", "tensor"), None),
        P(("dp", "tensor"), None),
        P(None, "dp", "tensor"),
        P("tensor", "dp"),
        P("dp", "tensor"),
        P("tensor", "dp"),
        P(None, ("tensor", "dp")),
        P(("tensor", "dp")),
        P(None, ("dp", "tensor")),
        P(None, ("dp", "tensor")),
    )
    return jax.shard_map(
        body,
        mesh=mesh,
        in_specs=placed,
        out_specs=(
            P(("dp", "tensor"), None),
            P(("dp", "tensor"), None),
            P(None, "dp", "tensor"),
            P("tensor", "dp"),
            P("dp", "tensor"),
            P("tensor", "dp"),
            P(None, ("tensor", "dp")),
            P(("tensor", "dp")),
            P(None, ("dp", "tensor")),
            P(None, ("dp", "tensor")),
        ),
        check_vma=False,
    )
```

profile of v0, /device:TPU:0, one launch (start us, length us, event | category | flops | bytes accessed | tf_op | source)
XLA Modules:
  0.0 749.5 jit_solution(3741249850792441844)
XLA Ops:
  10.5 43.2 %all-gather = bf16[32,24,2]{1,2,0:T(2,128)(2,1)S(1)} all-gather(bf16[1,24,2]{1,2,0:T(2,128)(2,1)} %bitcast.233), channel_id=1, replica_groups=mesh['dp'=8,'tensor'=4] {'dp','tensor'}, dimensions={0}, use_global_device_ids=true | all-gather | bytes 3168 | tf_op jit(solution)/shard_map/all_gather | solution.py:150
  54.1 36.9 %all-gather.1 = bf16[32,24,4]{1,2,0:T(4,128)(2,1)S(1)} all-gather(bf16[1,24,4]{1,2,0:T(4,128)(2,1)} %bitcast.232), channel_id=1, replica_groups=mesh['dp'=8,'tensor'=4] {'dp','tensor'}, dimensions={0}, use_global_device_ids=true | all-gather | bytes 6336 | tf_op jit(solution)/shard_map/all_gather | solution.py:151
  94.0 16.2 %all-gather.2 = bf16[8,24,2]{1,2,0:T(2,128)(2,1)S(1)} all-gather(bf16[1,24,2]{1,2,0:T(2,128)(2,1)S(1)} %bitcast.234), channel_id=1, replica_groups=mesh['dp'=8,'tensor'=4] {'dp'}, dimensions={0}, use_global_device_ids=true | all-gather | bytes 864 | tf_op jit(solution)/shard_map/all_gather | solution.py:58
  110.6 35.6 %all_gather.39 = bf16[3,768,192]{2,0,1:T(4,128)(2,1)S(1)} all-gather(bf16[3,96,192]{2,0,1:T(4,128)(2,1)S(1)} %copy.72), channel_id=1, replica_groups=mesh['dp'=8,'tensor'=4] {'dp'}, dimensions={1}, use_global_device_ids=true | all-gather | bytes 995328 | tf_op jit(solution)/shard_map/all_gather | solution.py:56
  147.2 31.0 %all_gather.41 = bf16[192,768]{0,1:T(8,128)(2,1)S(1)} all-gather(bf16[192,96]{0,1:T(8,128)(2,1)S(1)} %copy.79), channel_id=1, replica_groups=mesh['dp'=8,'tensor'=4] {'dp'}, dimensions={1}, use_global_device_ids=true | all-gather | bytes 331776 | tf_op jit(solution)/shard_map/all_gather | solution.py:57
  187.9 21.0 %while.54 = (s32[]{:T(128)}, bf16[3,1024,64]{1,2,0:T(8,128)(2,1)}, f32[3,1024]{1,0:T(4,128)}, bf16[3,1024,64]{2,1,0:T(8,128)(2,1)S(1)}, bf16[3,1024,64]{2,1,0:T(...) while((s32[]{:T(128)}, bf16[3,1024,64]{1,2,0:T(8,128)(2,1)}, ...), condition=%wide.region_7.8_spmd, body=%wide.region_2.7_spmd.sunk | while | flops 138935808 | bytes 8687918 | solution.py:179
  212.4 27.1 %reduce-scatter.16.cloned.1.call-done = bf16[256,768]{1,0:T(8,128)(2,1)} async-done(((bf16[1024,768]{1,0:T(8,128)(2,1)}), bf16[256,768]{1,0:T(8,128)(2,1)}) %reduce-scatter.16.cloned.1.call-update) | async-done | bytes 393232 | tf_op jit(solution)/shard_map/reduce_scatter | solution.py:49
  246.1 21.6 %all-reduce = bf16[768]{0:T(1024)(128)(2,1)S(1)} all-reduce(bf16[768]{0:T(1024)(128)(2,1)S(1)} %dynamic-update-slice), channel_id=1, replica_groups=mesh['dp'=8,'tensor'=4] {'dp'}, use_global_device_ids=true, to_apply=%add | all-reduce | flops 768 | bytes 3072
  267.7 8.2 %all-gather.12.cloned.1.call-done = bf16[1024,768]{1,0:T(8,128)(2,1)} async-done(((bf16[256,768]{1,0:T(8,128)(2,1)}), bf16[1024,768]{1,0:T(8,128)(2,1)}) %all-gather.12.cloned.1.call-update) | async-done | bytes 1572880 | tf_op jit(solution)/shard_map/all_gather | solution.py:45
  275.8 5.4 multiply_convert_fusion.1
  281.2 38.4 %all-gather.16.cloned.1.call-done = bf16[768,768]{0,1:T(8,128)(2,1)} async-done(((bf16[768,96]{0,1:T(8,128)(2,1)}), bf16[768,768]{0,1:T(8,128)(2,1)}) %all-gather.16.cloned.1.call-update) | async-done | bytes 1179664 | tf_op jit(solution)/shard_map/all_gather | solution.py:65
  319.7 19.7 %all-gather.18.cloned.1.call-done = bf16[1024,768]{1,0:T(8,128)(2,1)} async-done(((bf16[256,768]{1,0:T(8,128)(2,1)}), bf16[1024,768]{1,0:T(8,128)(2,1)}) %all-gather.18.cloned.1.call-update) | async-done | bytes 1572880 | tf_op jit(solution)/shard_map/all_gather | solution.py:45
  339.3 5.5 convert_reduce_fusion
  353.1 23.9 %reduce-scatter.20.cloned.1.call-done = bf16[256,768]{1,0:T(8,128)(2,1)} async-done(((bf16[1024,768]{1,0:T(8,128)(2,1)}), bf16[256,768]{1,0:T(8,128)(2,1)}) %reduce-scatter.20.cloned.1.call-update) | async-done | bytes 393232 | tf_op jit(solution)/shard_map/reduce_scatter | solution.py:49
  380.2 27.4 %reduce-scatter.18.cloned.1.call-done = bf16[256,768]{1,0:T(8,128)(2,1)} async-done(((bf16[1024,768]{1,0:T(8,128)(2,1)}), bf16[256,768]{1,0:T(8,128)(2,1)}) %reduce-scatter.18.cloned.1.call-update) | async-done | bytes 393232 | tf_op jit(solution)/shard_map/reduce_scatter | solution.py:49
  411.6 19.5 %all-gather.20.cloned.1.call-done = bf16[1024,768]{1,0:T(8,128)(2,1)} async-done(((bf16[256,768]{1,0:T(8,128)(2,1)}), bf16[1024,768]{1,0:T(8,128)(2,1)}) %all-gather.20.cloned.1.call-update) | async-done | bytes 1572880 | tf_op jit(solution)/shard_map/all_gather | solution.py:45
  437.7 31.2 %while.56 = (s32[]{:T(128)}, bf16[3,1024,64]{2,1,0:T(8,128)(2,1)}, bf16[3,1024,64]{1,2,0:T(8,128)(2,1)}, bf16[3,1024,64]{1,2,0:T(8,128)(2,1)}, bf16[3,1024,64]{2...) while((s32[]{:T(128)}, bf16[3,1024,64]{2,1,0:T(8,128)(2,1)}, ...), condition=%wide.region_19.20_spmd, body=%wide.region_15.19_spmd.sunk | while | flops 340262400 | bytes 20670868 | solution.py:225
  461.3 5.4 while.58
  495.8 21.6 %all-reduce.6 = (f32[2,192]{1,0:T(2,128)S(1)}, f32[768]{0:T(1024)S(1)}) all-reduce(f32[2,192]{1,0:T(2,128)S(1)} %pad_maximum_fusion.5, f32[768]{0:T(1024)S(1)} %copy-done.22), channel_id=10, replica_groups=mesh['dp'=8,'tensor'=4] {'dp'}, use_global_device_ids=true, to_apply=%region_29.30.clone | all-reduce | flops 1152 | bytes 9216
  520.3 6.7 reduce-scatter.22.cloned.1.call-done
  528.5 40.3 %all-reduce.5 = (f32[2,768]{1,0:T(2,128)S(1)}, f32[4,768]{1,0:T(4,128)S(1)}) all-reduce(f32[2,768]{1,0:T(2,128)S(1)} %pad_maximum_fusion.4, f32[4,768]{1,0:T(4,128)S(1)} %pad_maximum_fusion.3), channel_id=12, replica_groups=mesh['dp'=8,'tensor'=4] {'dp','tensor'}, use_global_device_ids=true, to_apply=%region_34.35.clone | all-reduce | flops 4608 | bytes 36864
  572.3 25.5 %reduce-scatter.28.cloned.1.call-done = f32[96,576]{1,0:T(8,128)} async-done(((f32[768,576]{1,0:T(8,128)}), f32[96,576]{1,0:T(8,128)}) %reduce-scatter.28.cloned.1.call-update) | async-done | bytes 221200
  599.7 70.4 %reduce-scatter.24.cloned.1.call-done = f32[96,768]{1,0:T(8,128)} async-done(((f32[768,768]{1,0:T(8,128)}), f32[96,768]{1,0:T(8,128)}) %reduce-scatter.24.cloned.1.call-update) | async-done | bytes 294928 | tf_op jit(solution)/shard_map/reduce_scatter | solution.py:208
  670.1 72.3 %reduce-scatter.26.cloned.1.call-done = f32[768,96]{0,1:T(8,128)} async-done(((f32[768,768]{0,1:T(8,128)}), f32[768,96]{0,1:T(8,128)}) %reduce-scatter.26.cloned.1.call-update) | async-done | bytes 294928 | tf_op jit(solution)/shard_map/reduce_scatter | solution.py:209
  (318 shorter events, 156.3 us)
Async XLA Ops:
  8.0 85.9 %copy-start.24 = (bf16[2,24]{1,0:T(2,128)(2,1)S(1)}, bf16[2,24]{1,0:T(2,128)(2,1)}, u32[]{:S(2)}) copy-start(bf16[2,24]{1,0:T(2,128)(2,1)} %param.24) | copy-start | bytes 292
  8.0 102.4 %copy-start.12 = (bf16[192,96]{1,0:T(8,128)(2,1)S(1)}, bf16[192,96]{1,0:T(8,128)(2,1)}, u32[]{:S(2)}) copy-start(bf16[192,96]{1,0:T(8,128)(2,1)} %param.21) | copy-start | bytes 110596
  8.0 102.5 %copy-start.9 = (bf16[3,96,192]{2,1,0:T(8,128)(2,1)S(1)}, bf16[3,96,192]{2,1,0:T(8,128)(2,1)}, u32[]{:S(2)}) copy-start(bf16[3,96,192]{2,1,0:T(8,128)(2,1)} %param.20) | copy-start | bytes 331780
  8.0 170.1 %all-gather.10.cloned.1.call-start = ((), (), s32[]{:S(2)}) async-start(), calls=%async_computation.8 | async-start | bytes 1966080 | tf_op jit(solution)/shard_map/all_gather | solution.py:45
  9.3 137.0 %copy-start.13 = (f32[256]{0:T(256)}, f32[256]{0:T(256)S(1)}, u32[]{:S(2)}) copy-start(f32[256]{0:T(256)S(1)} %broadcast_multiply_fusion.5) | copy-start | bytes 3076
  10.5 135.8 %copy-start.15 = (f32[256]{0:T(256)}, f32[256]{0:T(256)S(1)}, u32[]{:S(2)}) copy-start(f32[256]{0:T(256)S(1)} %add_rsqrt_fusion.1) | copy-start | bytes 3076
  54.0 92.3 %copy-start.10 = (f32[768]{0:T(1024)}, f32[768]{0:T(1024)S(1)}, u32[]{:S(2)}) copy-start(f32[768]{0:T(1024)S(1)} %get-tuple-element.297) | copy-start | bytes 9220
  93.9 145.7 %reduce-scatter.16.cloned.1.call-start = ((), (), s32[]{:S(2)}) async-start(), calls=%async_computation.9 | async-start | bytes 1966080 | tf_op jit(solution)/shard_map/reduce_scatter | solution.py:49
  147.2 33.5 %copy-start.7 = (bf16[3,768,192]{1,2,0:T(8,128)(2,1)}, bf16[3,768,192]{1,2,0:T(8,128)(2,1)S(1)}, u32[]{:S(2)}) copy-start(bf16[3,768,192]{1,2,0:T(8,128)(2,1)S(1)} %copy.73) | copy-start | bytes 2654212
  211.8 55.8 %all-gather.14.cloned.1.call-start = ((), (), s32[]{:S(2)}) async-start(), calls=%async_computation.11 | async-start | bytes 1327104 | tf_op jit(solution)/shard_map/all_gather | solution.py:64
  212.4 63.4 %all-gather.12.cloned.1.call-start = ((), (), s32[]{:S(2)}) async-start(), calls=%async_computation.10 | async-start | bytes 1966080 | tf_op jit(solution)/shard_map/all_gather | solution.py:45
  243.2 76.5 %all-gather.16.cloned.1.call-start = ((), (), s32[]{:S(2)}) async-start(), calls=%async_computation.12 | async-start | bytes 1327104 | tf_op jit(solution)/shard_map/all_gather | solution.py:65
  243.8 95.6 %all-gather.18.cloned.1.call-start = ((), (), s32[]{:S(2)}) async-start(), calls=%async_computation.14 | async-start | bytes 1966080 | tf_op jit(solution)/shard_map/all_gather | solution.py:45
  244.5 132.4 %reduce-scatter.20.cloned.1.call-start = ((), (), s32[]{:S(2)}) async-start(), calls=%async_computation.15 | async-start | bytes 1966080 | tf_op jit(solution)/shard_map/reduce_scatter | solution.py:49
  348.6 58.9 %reduce-scatter.18.cloned.1.call-start = ((), (), s32[]{:S(2)}) async-start(), calls=%async_computation.13 | async-start | bytes 1966080 | tf_op jit(solution)/shard_map/reduce_scatter | solution.py:49
  353.0 78.1 %all-gather.20.cloned.1.call-start = ((), (), s32[]{:S(2)}) async-start(), calls=%async_computation.16 | async-start | bytes 1966080 | tf_op jit(solution)/shard_map/all_gather | solution.py:45
  411.5 107.2 %reduce-scatter.30.cloned.1.call-start = ((), (), s32[]{:S(2)}) async-start(), calls=%async_computation.21 | async-start | bytes 884736
  434.2 92.8 %reduce-scatter.22.cloned.1.call-start = ((), (), s32[]{:S(2)}) async-start(), calls=%async_computation.17 | async-start | bytes 1966080 | tf_op jit(solution)/shard_map/reduce_scatter | solution.py:49
  474.5 123.3 %reduce-scatter.28.cloned.1.call-start = ((), (), s32[]{:S(2)}) async-start(), calls=%async_computation.20 | async-start | bytes 2211840
  483.7 186.3 %reduce-scatter.24.cloned.1.call-start = ((), (), s32[]{:S(2)}) async-start(), calls=%async_computation.18 | async-start | bytes 2654208 | tf_op jit(solution)/shard_map/reduce_scatter | solution.py:208
  489.5 252.8 %reduce-scatter.26.cloned.1.call-start = ((), (), s32[]{:S(2)}) async-start(), calls=%async_computation.19 | async-start | bytes 2654208 | tf_op jit(solution)/shard_map/reduce_scatter | solution.py:209
  493.8 33.2 %copy-start.1 = (bf16[256,768]{1,0:T(8,128)(2,1)S(1)}, bf16[256,768]{1,0:T(8,128)(2,1)}, u32[]{:S(2)}) copy-start(bf16[256,768]{1,0:T(8,128)(2,1)} %param.18) | copy-start | bytes 1179652
  493.8 33.2 %copy-start.11 = (f32[768]{0:T(1024)S(1)}, f32[768]{0:T(1024)}, u32[]{:S(2)}) copy-start(f32[768]{0:T(1024)} %copy-done.10) | copy-start | bytes 9220
  493.8 76.3 %copy-start.4 = (f32[256,768]{1,0:T(8,128)S(1)}, f32[256,768]{1,0:T(8,128)}, u32[]{:S(2)}) copy-start(f32[256,768]{1,0:T(8,128)} %copy-done.3) | copy-start | bytes 2359300
  (23 other events, 214.2 us)
Sparse Core Ops, SparseCore 0:
  94.0 17.1 all-gather.9
  211.9 27.6 reduce-scatter.15
  348.7 28.1 reduce-scatter.19
  379.3 28.1 reduce-scatter.17
Sparse Core Ops, SparseCore 1:
  214.7 40.9 all-gather.13
  257.8 18.0 all-gather.11
  278.1 41.5 all-gather.15
  321.3 18.0 all-gather.17
  411.6 19.5 all-gather.19
  434.8 62.6 reduce-scatter.29
  499.8 27.1 reduce-scatter.21
  530.7 67.0 reduce-scatter.27
  601.8 68.2 reduce-scatter.23
  674.1 68.1 reduce-scatter.25
where the time goes:
time: 751 us; the launch traced here: 749 us
  waiting for transfers between devices  341 us (45%)
  blocking collectives  246 us (33%)
  matrix products  63.5 us (8%)
  local copies, waits for them, and re-layouts  48.8 us (6%)
  other arithmetic  30.3 us (4%)
  between operations  18 us (2%)
    reduce_scatter x4, waiting for transfers between devices, reduce_frames(): lax.psum_scatter(partial_sum.astype(jnp.bfloat16), 'tensor', scatter_dime...  85 us
    unnamed x3, blocking collectives  83.4 us
    reduce_scatter x1, waiting for transfers between devices, body(): lax.psum_scatter(down_grad, 'dp', scatter_dimension=1, tiled=True)  72.3 us
    reduce_scatter x1, waiting for transfers between devices, body(): lax.psum_scatter(up_grad, 'dp', scatter_dimension=0, tiled=True)  70.4 us
    all_gather x4, waiting for transfers between devices, spread_frames(): return lax.all_gather(piece, 'tensor', axis=0, tiled=True)  47.4 us
    all_gather x1, blocking collectives, body(): lax.all_gather(norm_gains, ('dp', 'tensor'), axis=1, tiled=True)  43.2 us
    all_gather x1, waiting for transfers between devices, fetch_mlp(): lax.all_gather(down_weight, 'dp', axis=1, tiled=True)  38.4 us
    all_gather x1, blocking collectives, body(): lax.all_gather(row_biases, ('dp', 'tensor'), axis=1, tiled=True)  36.9 us
  transfers between devices with their start and end apart: 14, of which 11 were waited for; matrix products, arithmetic and copies ran while one was open for 11% of the time, Pallas kernels for 0%

commit v1 on v0

v1 whole, which is shorter than its diff:
```python
import functools

import jax
import jax.numpy as jnp
from jax import lax
from jax.experimental import pallas as pl
from jax.experimental.pallas import tpu as pltpu
from jax.sharding import PartitionSpec as P

HD = 64
EPSILON = 1e-05
SCALE = 0.125
ROOT_HALF = 0.7071067811865476
ROOT_TWO_PI_INVERSE = 0.3989422804014327
F32 = jnp.float32
BF16 = jnp.bfloat16
VMEM_LIMIT = 50 * 1024 * 1024
MESH = pl.DeviceIdType.MESH
TENSOR = 4


def layer_norm(values, gain_row, shift_row):
    center = values - jnp.mean(values, axis=-1, keepdims=True)
    spread = jnp.mean(center * center, axis=-1, keepdims=True)
    return center * lax.rsqrt(spread + EPSILON) * gain_row + shift_row


def norm_back(values, gain_row, incoming):
    center = values - jnp.mean(values, axis=-1, keepdims=True)
    spread = jnp.mean(center * center, axis=-1, keepdims=True)
    inverse = lax.rsqrt(spread + EPSILON)
    unit_rows = center * inverse
    scaled = incoming * gain_row
    grad_in = inverse * (
        scaled
        - jnp.mean(scaled, axis=-1, keepdims=True)
        - unit_rows * jnp.mean(scaled * unit_rows, axis=-1, keepdims=True)
    )
    return (
        grad_in,
        jnp.sum(incoming * unit_rows, axis=0, keepdims=True),
        jnp.sum(incoming, axis=0, keepdims=True),
    )


class Place:
    def __init__(self, dp):
        self.dp = dp
        self.zs = dp // 2
        self.d = lax.axis_index("dp")
        self.t = lax.axis_index("tensor")
        self.z = self.d // 2
        self.x = lax.rem(self.d, 2)
        self.core = self.t + 1 - 2 * lax.rem(self.t, 2)
        self.across = lax.rem(self.t + 2, TENSOR)
        self.diagonal = lax.rem(self.core + 2, TENSOR)

    def tensor_id(self, t):
        return {"dp": self.d, "tensor": t}

    def dp_id(self, d):
        return {"dp": d, "tensor": self.t}

    def x_id(self):
        return self.dp_id(self.z * 2 + 1 - self.x)

    def z_of(self, k):
        return lax.rem(self.z + k, self.zs)

    def z_from(self, k):
        return lax.rem(self.z + self.zs - k, self.zs)

    def z_id(self, k):
        return self.dp_id(self.z_of(k) * 2 + self.x)


def greet(peers):
    barrier = pltpu.get_barrier_semaphore()
    for peer in peers:
        pl.semaphore_signal(barrier, inc=1, device_id=peer, device_id_type=MESH)
    pl.semaphore_wait(barrier, len(peers))


def remote(src, dst, send, recv, peer):
    return pltpu.make_async_remote_copy(
        src_ref=src, dst_ref=dst, send_sem=send, recv_sem=recv, device_id=peer, device_id_type=MESH
    )


class TensorGather:
    def __init__(self, here, own, out, send, recv):
        t = here.t
        self.first = [
            remote(own, out.at[t], send.at[0], recv.at[0], here.tensor_id(here.across)),
            remote(own, out.at[t], send.at[1], recv.at[1], here.tensor_id(here.core)),
        ]
        landed = out.at[here.across]
        self.relay = remote(landed, landed, send.at[2], recv.at[2], here.tensor_id(here.core))

    def start(self):
        for copy in self.first:
            copy.start()

    def pass_on(self):
        self.first[0].wait_recv()
        self.relay.start()

    def finish(self):
        self.first[1].wait_recv()
        self.relay.wait_recv()
        self.first[0].wait_send()
        self.first[1].wait_send()
        self.relay.wait_send()


class TensorScatter:
    def __init__(self, here, part, from_core, to_across, from_across, send, recv):
        self.here, self.part = here, part
        self.from_core, self.to_across, self.from_across = from_core, to_across, from_across
        core = here.tensor_id(here.core)
        self.far = remote(part.at[here.diagonal], from_core.at[0], send.at[0], recv.at[0], core)
        self.near = remote(part.at[here.core], from_core.at[1], send.at[1], recv.at[1], core)
        self.cross = remote(
            to_across, from_across, send.at[2], recv.at[2], here.tensor_id(here.across)
        )

    def start(self):
        self.far.start()
        self.near.start()

    def pass_on(self):
        self.far.wait_recv()
        total = self.part[self.here.across].astype(F32) + self.from_core[0].astype(F32)
        self.to_across[...] = total.astype(BF16)
        self.cross.start()

    def result(self):
        self.near.wait_recv()
        total = self.part[self.here.t].astype(F32) + self.from_core[1].astype(F32)
        self.cross.wait_recv()
        return total + self.from_across[...].astype(F32)

    def finish(self):
        self.far.wait_send()
        self.near.wait_send()
        self.cross.wait_send()


def scatter_scratch(rows, width):
    return [
        pltpu.VMEM((2, rows, width), BF16),
        pltpu.VMEM((rows, width), BF16),
        pltpu.VMEM((rows, width), BF16),
        pltpu.SemaphoreType.DMA((3,)),
        pltpu.SemaphoreType.DMA((3,)),
    ]


class WeightGather:
    def __init__(self, here, own, out, sz, rz, sx, rx, local):
        self.zs = here.zs
        mine = out.at[here.z, here.x]
        self.keep = pltpu.make_async_copy(own, mine, local)
        self.along = [None] + [
            remote(own, mine, sz.at[k], rz.at[k], here.z_id(k)) for k in range(1, self.zs)
        ]
        self.over = [remote(own, mine, sx.at[0], rx.at[0], here.x_id())]
        for k in range(1, self.zs):
            landed = out.at[here.z_from(k), here.x]
            self.over.append(remote(landed, landed, sx.at[k], rx.at[k], here.x_id()))

    def start(self):
        for copy in self.along[1:]:
            copy.start()
        self.over[0].start()
        self.keep.start()

    def pass_on(self, k):
        self.along[k].wait_recv()
        self.over[k].start()

    def finish(self):
        for copy in self.over:
            copy.wait_recv()
        for copy in self.along[1:] + self.over:
            copy.wait_send()
        self.keep.wait()


def weight_sems(zs):
    return [pltpu.SemaphoreType.DMA((zs,))] * 4 + [pltpu.SemaphoreType.DMA]


class GradScatter:
    def __init__(self, here, part, from_x, to_z, from_z, sz, rz, sx, rx):
        self.here, self.part = here, part
        self.from_x, self.to_z, self.from_z = from_x, to_z, from_z
        self.order = list(range(1, here.zs)) + [0]
        self.over, self.along = {}, {}
        for k in self.order:
            slot = here.z_of(k)
            self.over[k] = remote(
                part.at[slot, 1 - here.x], from_x.at[k], sx.at[k], rx.at[k], here.x_id()
            )
            if k:
                self.along[k] = remote(to_z.at[k], from_z.at[k], sz.at[k], rz.at[k], here.z_id(k))

    def start(self):
        for k in self.order:
            self.over[k].start()

    def half(self, k):
        here = self.here
        self.over[k].wait_recv()
        return self.part[here.z_of(k), here.x].astype(F32) + self.from_x[k].astype(F32)

    def pass_on(self, k):
        self.to_z[k] = self.half(k).astype(BF16)
        self.along[k].start()

    def result(self):
        total = self.half(0)
        for k in range(1, self.here.zs):
            self.along[k].wait_recv()
            total = total + self.from_z[k].astype(F32)
        return total

    def finish(self):
        for k in self.order:
            self.over[k].wait_send()
            if k:
                self.along[k].wait_send()


def grad_scratch(zs, rows, width):
    return [pltpu.VMEM((zs, rows, width), BF16)] * 3 + [pltpu.SemaphoreType.DMA((zs,))] * 4


def tensor_peers(here):
    return [here.tensor_id(t) for t in (here.core, here.across, here.diagonal)]


def dp_peers(here):
    return [here.dp_id(lax.rem(here.d + k, here.dp)) for k in range(1, here.dp)]


def gather_kernel(dp, x_ref, c_ref, wa_ref, wb_ref, s_ref, x_out, c_out, wa_out, wb_out, s_out, *sems):
    here = Place(dp)
    gx = sems[0:2]
    gc = sems[2:4]
    wa = sems[4:9]
    wb = sems[9:14]
    st_send, st_recv, sd_send, sd_recv, local = sems[14:19]
    greet(tensor_peers(here) + dp_peers(here))
    keeps = [
        pltpu.make_async_copy(x_ref, x_out.at[here.t], local.at[0]),
        pltpu.make_async_copy(c_ref, c_out.at[here.t], local.at[1]),
        pltpu.make_async_copy(s_ref, s_out.at[here.d, here.t], local.at[2]),
    ]
    for copy in keeps:
        copy.start()
    small = [
        remote(s_ref, s_out.at[here.d, here.t], st_send.at[i], st_recv.at[i], peer)
        for i, peer in enumerate(tensor_peers(here))
    ]
    for copy in small:
        copy.start()
    x_gather = TensorGather(here, x_ref, x_out, *gx)
    x_gather.start()
    a_gather = WeightGather(here, wa_ref, wa_out, *wa)
    a_gather.start()
    for copy in small:
        copy.wait_recv()
    keeps[2].wait()
    row = s_out.at[here.d]
    spread = [
        remote(row, row, sd_send.at[k], sd_recv.at[k], here.dp_id(lax.rem(here.d + k, dp)))
        for k in range(1, dp)
    ]
    for copy in spread:
        copy.start()
    b_gather = WeightGather(here, wb_ref, wb_out, *wb)
    b_gather.start()
    c_gather = TensorGather(here, c_ref, c_out, *gc)
    c_gather.start()
    x_gather.pass_on()
    for k in range(1, here.zs):
        a_gather.pass_on(k)
    c_gather.pass_on()
    for k in range(1, here.zs):
        b_gather.pass_on(k)
    x_gather.finish()
    c_gather.finish()
    a_gather.finish()
    b_gather.finish()
    for copy in spread:
        copy.wait_recv()
    for copy in small + spread:
        copy.wait_send()
    keeps[0].wait()
    keeps[1].wait()


def gather_all(dp, x, cot, wa, wb, small):
    zs = dp // 2
    anywhere = pl.BlockSpec(memory_space=pl.ANY)
    dma = pltpu.SemaphoreType.DMA
    shape = jax.ShapeDtypeStruct
    return pl.pallas_call(
        functools.partial(gather_kernel, dp),
        out_shape=(
            shape((TENSOR,) + x.shape, BF16),
            shape((TENSOR,) + x.shape, BF16),
            shape((zs, 2) + wa.shape, BF16),
            shape((zs, 2) + wb.shape, BF16),
            shape((dp, TENSOR) + small.shape, BF16),
        ),
        in_specs=[anywhere] * 5,
        out_specs=(anywhere,) * 5,
        scratch_shapes=[dma((3,))] * 4
        + weight_sems(zs) * 2
        + [dma((3,)), dma((3,)), dma((dp,)), dma((dp,)), dma((3,))],
        compiler_params=pltpu.CompilerParams(
            collective_id=0, has_side_effects=True, vmem_limit_bytes=VMEM_LIMIT
        ),
    )(x, cot, wa, wb, small)


def middle_kernel(dp, part, x_ref, vec, middle_out, two_out, *rest):
    here = Place(dp)
    scatter = TensorScatter(here, part, *rest[0:5])
    gather = TensorGather(here, two_out.at[here.t], two_out, *rest[5:7])
    greet(tensor_peers(here))
    scatter.start()
    scatter.pass_on()
    middle = x_ref[...].astype(F32) + scatter.result() + vec[3:4]
    middle_out[...] = middle
    two_out[here.t] = layer_norm(middle, vec[1:2], vec[4:5]).astype(BF16)
    gather.start()
    gather.pass_on()
    gather.finish()
    scatter.finish()


def make_middle(dp, part, x, vec):
    vmem = pl.BlockSpec(memory_space=pltpu.VMEM)
    rows, width = x.shape
    dma = pltpu.SemaphoreType.DMA
    return pl.pallas_call(
        functools.partial(middle_kernel, dp),
        out_shape=(
            jax.ShapeDtypeStruct((rows, width), F32),
            jax.ShapeDtypeStruct((TENSOR, rows, width), BF16),
        ),
        in_specs=[vmem] * 3,
        out_specs=(vmem,) * 2,
        scratch_shapes=scatter_scratch(rows, width) + [dma((3,)), dma((3,))],
        compiler_params=pltpu.CompilerParams(
            collective_id=1, has_side_effects=True, vmem_limit_bytes=VMEM_LIMIT
        ),
    )(part, x, vec)


def back_kernel(dp, grad_part, feed_part, middle, cot, vec, out, mgrad_out, attn_out, sums, *rest):
    here = Place(dp)
    grad_scatter = TensorScatter(here, grad_part, *rest[0:5])
    feed_scatter = TensorScatter(here, feed_part, *rest[5:10])
    gather = TensorGather(here, attn_out.at[here.t], attn_out, *rest[10:12])
    greet(tensor_peers(here))
    grad_scatter.start()
    feed_scatter.start()
    grad_scatter.pass_on()
    incoming = grad_scatter.result()
    mid = middle[...]
    part, gain_sum, shift_sum = norm_back(mid, vec[1:2], incoming)
    grad_out = cot[...].astype(F32)
    mgrad = grad_out + part
    attn_out[here.t] = mgrad.astype(BF16)
    gather.start()
    feed_scatter.pass_on()
    mgrad_out[...] = mgrad
    sums[0:1] = gain_sum
    sums[1:2] = jnp.sum(mgrad, axis=0, keepdims=True)
    sums[2:3] = shift_sum
    sums[3:4] = jnp.sum(grad_out, axis=0, keepdims=True)
    gather.pass_on()
    out[...] = (mid + feed_scatter.result() + vec[5:6]).astype(BF16)
    gather.finish()
    grad_scatter.finish()
    feed_scatter.finish()


def go_back(dp, grad_part, feed_part, middle, cot, vec):
    vmem = pl.BlockSpec(memory_space=pltpu.VMEM)
    rows, width = cot.shape
    dma = pltpu.SemaphoreType.DMA
    shape = jax.ShapeDtypeStruct
    return pl.pallas_call(
        functools.partial(back_kernel, dp),
        out_shape=(
            shape((rows, width), BF16),
            shape((rows, width), F32),
            shape((TENSOR, rows, width), BF16),
            shape((4, width), F32),
        ),
        in_specs=[vmem] * 5,
        out_specs=(vmem,) * 4,
        scratch_shapes=scatter_scratch(rows, width) * 2 + [dma((3,)), dma((3,))],
        compiler_params=pltpu.CompilerParams(
            collective_id=2, has_side_effects=True, vmem_limit_bytes=VMEM_LIMIT
        ),
    )(grad_part, feed_part, middle, cot, vec)


def last_kernel(
    dp, part, x_ref, mgrad, vec, sums, own_sums, ga, gb,
    in_out, ga_out, gb_out, sum_out, *rest
):
    here = Place(dp)
    scatter = TensorScatter(here, part, *rest[0:5])
    a_scatter = GradScatter(here, ga, *rest[5:12])
    b_scatter = GradScatter(here, gb, *rest[12:19])
    near, around, st_send, st_recv, sd_send, sd_recv = rest[19:25]
    greet(tensor_peers(here) + dp_peers(here))
    scatter.start()
    b_scatter.start()
    a_scatter.start()
    scatter.pass_on()
    x = x_ref[...].astype(F32)
    in_part, gain_sum, shift_sum = norm_back(x, vec[0:1], scatter.result())
    in_out[...] = mgrad[...] + in_part
    near[0, 0:1] = gain_sum
    near[0, 1:2] = sums[0:1]
    near[0, 2:3] = shift_sum
    near[0, 3:6] = sums[1:4]
    near[0, 6:8] = jnp.zeros_like(near[0, 6:8])
    small = [
        remote(near.at[0], near.at[i + 1], st_send.at[i], st_recv.at[i], peer)
        for i, peer in enumerate(tensor_peers(here))
    ]
    for copy in small:
        copy.start()
    for k in range(1, here.zs):
        b_scatter.pass_on(k)
    for copy in small:
        copy.wait_recv()
    around[0, 0:8] = (near[0] + near[1]) + (near[2] + near[3])
    around[0, 8:16] = own_sums[...]
    spread = [
        remote(
            around.at[0], around.at[k], sd_send.at[k], sd_recv.at[k],
            here.dp_id(lax.rem(here.d + k, dp)),
        )
        for k in range(1, dp)
    ]
    for copy in spread:
        copy.start()
    for k in range(1, here.zs):
        a_scatter.pass_on(k)
    gb_out[...] = b_scatter.result()
    total = around[0]
    for k in range(1, dp):
        spread[k - 1].wait_recv()
        total = total + around[k]
    sum_out[...] = total
    ga_out[...] = a_scatter.result()
    scatter.finish()
    a_scatter.finish()
    b_scatter.finish()
    for copy in small + spread:
        copy.wait_send()


def finish_all(dp, part, x, mgrad, vec, sums, own_sums, ga, gb):
    zs = dp // 2
    vmem = pl.BlockSpec(memory_space=pltpu.VMEM)
    rows, width = x.shape
    dma = pltpu.SemaphoreType.DMA
    shape = jax.ShapeDtypeStruct
    return pl.pallas_call(
        functools.partial(last_kernel, dp),
        out_shape=(
            shape((rows, width), F32),
            shape(ga.shape[2:], F32),
            shape(gb.shape[2:], F32),
            shape((16, width), F32),
        ),
        in_specs=[vmem] * 8,
        out_specs=(vmem,) * 4,
        scratch_shapes=scatter_scratch(rows, width)
        + grad_scratch(zs, *ga.shape[2:])
        + grad_scratch(zs, *gb.shape[2:])
        + [pltpu.VMEM((TENSOR, 8, width), F32), pltpu.VMEM((dp, 16, width), F32)]
        + [dma((3,)), dma((3,)), dma((dp,)), dma((dp,))],
        compiler_params=pltpu.CompilerParams(
            collective_id=3, has_side_effects=True, vmem_limit_bytes=VMEM_LIMIT
        ),
    )(part, x, mgrad, vec, sums, own_sums, ga, gb)


def attend_kernel(q_ref, k_ref, v_ref, out_ref, log_ref):
    scores = (
        lax.dot_general(q_ref[0], k_ref[0], (((1,), (1,)), ((), ())), preferred_element_type=F32)
        * SCALE
    )
    top = jnp.max(scores, axis=1, keepdims=True)
    exponent = jnp.exp(scores - top)
    total = jnp.sum(exponent, axis=1, keepdims=True)
    probs = (exponent * (1.0 / total)).astype(BF16)
    out_ref[0] = jnp.dot(probs, v_ref[0], preferred_element_type=F32).astype(BF16)
    log_ref[0] = top + jnp.log(total)


def attend(q, k, v, block):
    heads, frames, width = q.shape
    some = pl.BlockSpec((1, block, width), lambda h, i: (h, i, 0))
    every = pl.BlockSpec((1, frames, width), lambda h, i: (h, 0, 0))
    return pl.pallas_call(
        attend_kernel,
        grid=(heads, frames // block),
        out_shape=(
            jax.ShapeDtypeStruct(q.shape, BF16),
            jax.ShapeDtypeStruct((heads, frames, 1), F32),
        ),
        in_specs=[some, every, every],
        out_specs=(some, pl.BlockSpec((1, block, 1), lambda h, i: (h, i, 0))),
        compiler_params=pltpu.CompilerParams(vmem_limit_bytes=VMEM_LIMIT),
    )(q, k, v)


def attend_back_kernel(q_ref, g_ref, log_ref, k_ref, v_ref, dq_ref, dk_ref, dv_ref, dk_sum, dv_sum):
    step = pl.program_id(1)
    contract_last = (((1,), (1,)), ((), ()))
    contract_first = (((0,), (0,)), ((), ()))

    @pl.when(step == 0)
    def _():
        dk_sum[...] = jnp.zeros_like(dk_sum)
        dv_sum[...] = jnp.zeros_like(dv_sum)

    q, g, k, v = q_ref[0], g_ref[0], k_ref[0], v_ref[0]
    scores = lax.dot_general(q, k, contract_last, preferred_element_type=F32) * SCALE
    probs = jnp.exp(scores - log_ref[0])
    prob_grad = lax.dot_general(g, v, contract_last, preferred_element_type=F32)
    row_dot = jnp.sum(probs * prob_grad, axis=1, keepdims=True)
    score_grad = (probs * (prob_grad - row_dot)).astype(BF16)
    dq_ref[0] = (jnp.dot(score_grad, k, preferred_element_type=F32) * SCALE).astype(BF16)
    dk_sum[...] += lax.dot_general(score_grad, q, contract_first, preferred_element_type=F32)
    dv_sum[...] += lax.dot_general(
        probs.astype(BF16), g, contract_first, preferred_element_type=F32
    )

    @pl.when(step == pl.num_programs(1) - 1)
    def _():
        dk_ref[0] = (dk_sum[...] * SCALE).astype(BF16)
        dv_ref[0] = dv_sum[...].astype(BF16)


def attend_back(q, k, v, log, g, block):
    heads, frames, width = q.shape
    some = pl.BlockSpec((1, block, width), lambda h, i: (h, i, 0))
    every = pl.BlockSpec((1, frames, width), lambda h, i: (h, 0, 0))
    thin = pl.BlockSpec((1, block, 1), lambda h, i: (h, i, 0))
    return pl.pallas_call(
        attend_back_kernel,
        grid=(heads, frames // block),
        out_shape=(jax.ShapeDtypeStruct(q.shape, BF16),) * 3,
        in_specs=[some, some, thin, every, every],
        out_specs=(some, every, every),
        scratch_shapes=[pltpu.VMEM((frames, width), F32)] * 2,
        compiler_params=pltpu.CompilerParams(vmem_limit_bytes=VMEM_LIMIT),
    )(q, g, log, k, v)


def pad_rows(array, rows, axis):
    extra = rows - array.shape[axis]
    if extra == 0:
        return array
    widths = [(0, 0)] * array.ndim
    widths[axis] = (0, extra)
    return jnp.pad(array, widths)


def body(dp, inputs, cotangent, qkv_weight, proj_weight, up_weight, down_weight, qv_bias, up_bias, norm_gains, row_biases):
    zs = dp // 2
    rows, width = inputs.shape
    share = qkv_weight.shape[1]
    padded = -(-share // 16) * 16
    columns = qkv_weight.shape[2]
    hidden_width = up_weight.shape[1]
    heads = columns // HD
    frames = rows * TENSOR

    def wide(array):
        array = array.reshape(array.shape[0], -1)
        return jnp.pad(array, ((0, 0), (0, 128 - array.shape[1])))

    wa = jnp.concatenate([qkv_weight[0], qkv_weight[1], qkv_weight[2], proj_weight.T], axis=1)
    wb = jnp.concatenate([up_weight, down_weight.T], axis=1)
    bit = norm_gains.shape[1]
    small = jnp.concatenate(
        [wide(norm_gains), wide(row_biases), wide(qv_bias), wide(up_bias[None])], axis=0
    )
    small = pad_rows(small, 16, 0)
    x_all, cot_all, wa_all, wb_all, small_all = gather_all(
        dp, inputs, cotangent, pad_rows(wa, padded, 0), pad_rows(wb, padded, 0), small
    )

    def whole(array):
        return array[:, :, :share].reshape(width, array.shape[3])

    def split(array):
        return pad_rows(array.reshape(zs, 2, share, array.shape[1]), padded, 2)

    x_all = x_all.reshape(frames, width)
    cot_all = cot_all.reshape(frames, width)
    wa_all, wb_all = whole(wa_all), whole(wb_all)
    qkv_full, proj_t = wa_all[:, : 3 * columns], wa_all[:, 3 * columns :]
    up_full, down_t = wb_all[:, :hidden_width], wb_all[:, hidden_width:]
    small_all = small_all.astype(F32)
    tensor = lax.axis_index("tensor")
    vec = small_all[:, :, 0:8, :bit].transpose(2, 0, 1, 3).reshape(8, width)
    mine = lax.dynamic_index_in_dim(small_all, tensor, 1, keepdims=False)
    bits = qv_bias.shape[1]
    qv_full = mine[:, 6:8, :bits].transpose(1, 0, 2).reshape(2, columns)
    up_bias_full = mine[:, 8, : up_bias.shape[0]].reshape(hidden_width)

    normed = layer_norm(x_all.astype(F32), vec[0:1], vec[2:3]).astype(BF16)
    bias_row = jnp.concatenate([qv_full[0], jnp.zeros_like(qv_full[0]), qv_full[1]])
    projected = (jnp.dot(normed, qkv_full, preferred_element_type=F32) + bias_row).astype(BF16)
    split_qkv = projected.reshape(frames, 3, heads, HD).transpose(1, 2, 0, 3)
    head_q, head_k, head_v = split_qkv[0], split_qkv[1], split_qkv[2]

    def join_heads(stacked):
        return stacked.transpose(1, 0, 2).reshape(frames, columns)

    mixture, logsum = attend(head_q, head_k, head_v, min(512, frames))
    attended = join_heads(mixture)
    contract_last = (((1,), (1,)), ((), ()))
    contract_first = (((0,), (0,)), ((), ()))

    def blocks(array):
        return array.reshape(TENSOR, rows, width)

    branch = lax.dot_general(attended, proj_t, contract_last, preferred_element_type=F32)
    middle, normed_two = make_middle(dp, blocks(branch.astype(BF16)), inputs, vec)
    normed_two = normed_two.reshape(frames, width)
    hidden = jnp.dot(normed_two, up_full, preferred_element_type=F32) + up_bias_full
    cumulative = 0.5 * (1.0 + jax.scipy.special.erf(hidden * ROOT_HALF))
    activated = (hidden * cumulative).astype(BF16)
    slope = cumulative + hidden * jnp.exp(-0.5 * hidden * hidden) * ROOT_TWO_PI_INVERSE
    act_grad = jnp.dot(cot_all, down_t, preferred_element_type=F32)
    hidden_grad = (act_grad * slope).astype(BF16)
    grad_part = lax.dot_general(hidden_grad, up_full, contract_last, preferred_element_type=F32)
    feed_part = lax.dot_general(activated, down_t, contract_last, preferred_element_type=F32)
    outputs, middle_grad, attn_grad, sums = go_back(
        dp, blocks(grad_part.astype(BF16)), blocks(feed_part.astype(BF16)), middle, cotangent, vec
    )
    up_bias_grad = jnp.sum(hidden_grad.astype(F32), axis=0)
    up_grad = lax.dot_general(normed_two, hidden_grad, contract_first, preferred_element_type=F32)
    down_grad = lax.dot_general(cot_all, activated, contract_first, preferred_element_type=F32)
    attn_grad = attn_grad.reshape(frames, width)
    proj_grad = lax.dot_general(attn_grad, attended, contract_first, preferred_element_type=F32)
    attended_grad = jnp.dot(attn_grad, proj_t, preferred_element_type=F32).astype(BF16)
    head_g = attended_grad.reshape(frames, heads, HD).transpose(1, 0, 2)
    head_dq, head_dk, head_dv = attend_back(
        head_q, head_k, head_v, logsum, head_g, min(512, frames)
    )
    stacked = jnp.concatenate([join_heads(head_dq), join_heads(head_dk), join_heads(head_dv)], axis=1)
    qkv_grad = lax.dot_general(normed, stacked, contract_first, preferred_element_type=F32)
    column_sums = jnp.sum(stacked.astype(F32), axis=0)
    normed_part = lax.dot_general(stacked, qkv_full, contract_last, preferred_element_type=F32)
    own_sums = jnp.zeros((8, width), F32)
    own_sums = own_sums.at[0, :hidden_width].set(up_bias_grad)
    own_sums = own_sums.at[1, :columns].set(column_sums[:columns])
    own_sums = own_sums.at[2, :columns].set(column_sums[2 * columns :])
    ga = jnp.concatenate([qkv_grad, proj_grad], axis=1).astype(BF16)
    gb = jnp.concatenate([up_grad, down_grad], axis=1).astype(BF16)
    input_grad, ga_out, gb_out, all_sums = finish_all(
        dp, blocks(normed_part.astype(BF16)), inputs, middle_grad, vec, sums, own_sums, split(ga), split(gb)
    )
    ga_out, gb_out = ga_out[:share], gb_out[:share]
    place = lax.axis_index("dp")
    both = place * TENSOR + tensor
    qkv_grad_out = ga_out[:, : 3 * columns].reshape(share, 3, columns).transpose(1, 0, 2)
    vectors = lax.dynamic_slice(all_sums, (0, both * bit), (6, bit))
    qv_out = lax.dynamic_slice(all_sums, (9, place * bits), (2, bits))
    up_bits = up_bias.shape[0]
    up_bias_out = lax.dynamic_slice(all_sums, (8, place * up_bits), (1, up_bits))[0]
    return (
        outputs,
        input_grad,
        qkv_grad_out,
        ga_out[:, 3 * columns :].T,
        gb_out[:, :hidden_width],
        gb_out[:, hidden_width:].T,
        qv_out,
        up_bias_out,
        vectors[0:2],
        vectors[2:6],
    )


def solution(mesh):
    both = ("dp", "tensor")
    placed = (
        P(both, None),
        P(both, None),
        P(None, "dp", "tensor"),
        P("tensor", "dp"),
        P("dp", "tensor"),
        P("tensor", "dp"),
        P(None, ("tensor", "dp")),
        P(("tensor", "dp")),
        P(None, both),
        P(None, both),
    )
    return jax.shard_map(
        functools.partial(body, mesh.shape["dp"]),
        mesh=mesh,
        in_specs=placed,
        out_specs=(
            P(both, None),
            P(both, None),
            P(None, "dp", "tensor"),
            P("tensor", "dp"),
            P("dp", "tensor"),
            P("tensor", "dp"),
            P(None, ("tensor", "dp")),
            P(("tensor", "dp")),
            P(None, both),
            P(None, both),
        ),
        check_vma=False,
    )
```

time: 751 us -> 295 us (0.39)
  waiting for transfers between devices: 341 us -> 0 us
  blocking collectives: 246 us -> 0 us
  Pallas kernels: 0 us -> 210 us
  matrix products: 63.5 us -> 38.2 us
  other arithmetic: 30.3 us -> 7.73 us
  between operations: 18 us -> 1.15 us
  local copies, waits for them, and re-layouts: 48.8 us -> 36.2 us
    reduce_scatter x6 -> x0, waiting for transfers between devices: 228 us -> none  [the longest x4 85 us: reduce_frames(): lax.psum_scatter(partial_sum.astype(jnp.bfloat16), 'tensor', scatter_dime...]
    pallas_call x0 -> x6, Pallas kernels: none -> 210 us  [the longest x1 69.2 us: finish_all(): pl.pallas_call(functools.partial(last_kernel, dp), out_shape=(shape((rows...]
    all_gather x5 -> x0, blocking collectives: 163 us -> none  [the longest x1 43.2 us: body(): lax.all_gather(norm_gains, ('dp', 'tensor'), axis=1, tiled=True)]
    all_gather x6 -> x0, waiting for transfers between devices: 85.8 us -> none  [the longest x4 47.4 us: spread_frames(): return lax.all_gather(piece, 'tensor', axis=0, tiled=True)]
    unnamed x3 -> x0, blocking collectives: 83.4 us -> none
    unnamed x16 -> x0, waiting for transfers between devices: 27.4 us -> none
    dot_general x52 -> x12, matrix products: 58 us -> 38.2 us  [the longest x1 4.41 us: body(): lax.dot_general(normed_two, hidden_grad, contract_first, preferred_elemen...]
    reduce_sum x11 -> x1, other arithmetic: 10.2 us -> 0.24 us  [body(): column_sums = jnp.sum(stacked.astype(F32), axis=0)]
  transfers between devices with their start and end apart: 14 -> 0, of which waited for: 11 -> 0; matrix products, arithmetic and copies ran while one was open for 11% -> 0% of each run, Pallas kernels for 0% -> 0%
where the time goes in v1:
time: 295 us; the launch traced here: 293 us
  Pallas kernels  210 us (71%)
  matrix products  38.2 us (13%)
  local copies, waits for them, and re-layouts  36.2 us (12%)
  other arithmetic  7.73 us (3%)
    pallas_call x1, Pallas kernels, finish_all(): pl.pallas_call(functools.partial(last_kernel, dp), out_shape=(shape((rows...  69.2 us
    pallas_call x1, Pallas kernels, gather_all(): pl.pallas_call(functools.partial(gather_kernel, dp), out_shape=(shape((TE...  56.9 us
    pallas_call x1, Pallas kernels, go_back(): pl.pallas_call(functools.partial(back_kernel, dp), out_shape=(shape((rows...  34.4 us
    pallas_call x1, Pallas kernels, make_middle(): pl.pallas_call(functools.partial(middle_kernel, dp), out_shape=(jax.Shape...  26.5 us
    pallas_call x1, Pallas kernels, attend_back(): pl.pallas_call(attend_back_kernel, grid=(heads, frames // block), out_sha...  12.6 us
    unnamed x73, local copies, waits for them, and re-layouts  11.1 us
    pallas_call x1, Pallas kernels, attend(): pl.pallas_call(attend_kernel, grid=(heads, frames // block), out_shape=(j...  10.6 us

profile of v1, /device:TPU:0, one launch (start us, length us, event | category | flops | bytes accessed | tf_op | source)
XLA Modules:
  0.0 293.5 jit_solution(9586629760159063362)
XLA Ops:
  4.4 56.9 %shard_map.177 = (bf16[4,256,768]{2,1,0:T(8,128)(2,1)S(1)}, bf16[4,256,768]{2,1,0:T(8,128)(2,1)}, bf16[4,2,96,768]{3,2,1,0:T(8,128)(2,1)S(1)}, bf16[4,2,96,1536]...) custom-call(bf16[256,768]{1,0:T(8,128)(2,1)S(1)} %copy-done.2, bf16[256,768]{1,0:T(8,128)(2,1)S(1)} %copy-done.3, ...), custom_call_target="tpu_custom_call" | custom-call | tf_op jit(solution)/shard_map/pallas_call | solution.py:309
  63.7 1.8 fusion.9
  65.8 2.8 add_convert_fusion
  68.6 2.4 copy.29
  71.0 1.8 slice_bitcast_fusion
  72.8 10.6 %shard_map.178 = (bf16[3,1024,64]{2,1,0:T(8,128)(2,1)S(1)}, f32[3,1024,1]{2,1,0:T(8,128)}) custom-call(bf16[3,1024,64]{2,1,0:T(8,128)(2,1)S(1)} %get-tuple-element.112.q_ref, bf16[3,1024,64]{2,1,0:T(8,128)(2,1)S(1)} %get-tuple-element.111.k_ref, bf16[3,1024,64]{2,1,0:T(8,128)(2,1)S(1)} %get-tuple-element.110.v_ref), custom_call_target="tpu_custom_call" | custom-call | tf_op jit(solution)/shard_map/pallas_call | solution.py:518
  85.7 3.1 %convolution_convert_fusion.3 = bf16[1024,768]{1,0:T(8,128)(2,1)} fusion(bf16[1024,192]{0,1:T(8,128)(2,1)S(1)} %bitcast.139, bf16[768,768]{1,0:T(8,128)(2,1)} %bitcast.125), kind=kOutput, calls=%fused_computation.22 | convolution fusion | flops 302776320 | bytes 2359296 | tf_op jit(solution)/shard_map/dot_general | solution.py:645
  89.0 26.5 %shard_map.179 = (f32[256,768]{1,0:T(8,128)S(1)}, bf16[4,256,768]{2,1,0:T(8,128)(2,1)S(1)}) custom-call(bf16[4,256,768]{2,1,0:T(8,128)(2,1)} %bitcast.130, bf16[256,768]{1,0:T(8,128)(2,1)S(1)} %copy-done.2, f32[8,768]{1,0:T(8,128)S(1)} %reshape.219.vec), custom_call_target="tpu_custom_call" | custom-call | tf_op jit(solution)/shard_map/pallas_call | solution.py:349
  117.2 4.2 %multiply_convert_fusion = (bf16[1024,768]{1,0:T(8,128)(2,1)}, f32[1024,768]{1,0:T(8,128)S(1)}) fusion(f32[768]{0:T(1024)S(1)} %add.91, bf16[1024,768]{1,0:T(8,128)(2,1)S(1)} %bitcast.118, bf16[768,1536]{1,0:T(8,128)(2,1)} %bitcast.161), kind=kOutput, calls=%fused_computation.13 | convolution fusion | flops 1212678144 | bytes 7474176 | tf_op jit(solution)/shard_map/dot_general | solution.py:648
  121.4 3.8 %convert_reduce_fusion = (f32[768]{0:T(1024)S(1)}, bf16[1024,768]{1,0:T(8,128)(2,1)}) fusion(f32[1024,768]{1,0:T(8,128)S(1)} %get-tuple-element.123, f32[768]{0:T(1024)S(1)} %add.91, bf16[1024,768]{1,0:T(8,128)(2,1)S(1)} %bitcast.131, bf16[768,1536]{1,0:T(8,128)(2,1)S(1)} %bitcast.162), kind=kOutput, calls=%fused_computation.12 | convolution fusion | flops 1218182400 | bytes 7478272 | tf_op jit(solution)/shard_map/dot_general | solution.py:652
  125.2 1.7 copy.38
  126.9 4.4 %fusion.14 = bf16[4,2,96,768]{3,2,1,0:T(8,128)(2,1)} fusion(bf16[4,2,96,1024]{3,2,1,0:T(8,128)(2,1)} %bitcast.136, bf16[1024,768]{1,0:T(8,128)(2,1)} %get-tuple-element.125), kind=kOutput, calls=%fused_computation.28 | convolution fusion | flops 1208549376 | bytes 4325376 | tf_op jit(solution)/shard_map/dot_general | solution.py:660
  131.3 1.7 copy.39
  133.0 3.4 %fusion.17 = bf16[4,2,96,768]{3,2,1,0:T(8,128)(2,1)S(1)} fusion(bf16[4,2,96,1024]{3,2,1,0:T(8,128)(2,1)} %bitcast.137, bf16[1024,768]{1,0:T(8,128)(2,1)} %get-tuple-element.122), kind=kOutput, calls=%fused_computation.29 | convolution fusion | flops 1208549376 | bytes 4325376 | tf_op jit(solution)/shard_map/dot_general | solution.py:661
  139.3 2.7 convolution_convert_fusion.1
  142.0 2.6 convolution_convert_fusion.2
  144.6 34.4 %shard_map.180 = (bf16[256,768]{1,0:T(8,128)(2,1)S(1)}, f32[256,768]{1,0:T(8,128)S(1)}, bf16[4,256,768]{2,1,0:T(8,128)(2,1)S(1)}, f32[4,768]{1,0:T(4,128)S(1)}) custom-call(bf16[4,256,768]{2,1,0:T(8,128)(2,1)} %bitcast.134, bf16[4,256,768]{2,1,0:T(8,128)(2,1)} %bitcast.133, f32[256,768]{1,0:T(8,128)S(1)} %copy-done.12, bf16[256,768]{1,0:T(8,128)(2,1)S(1)} %copy-done.3, ...), custom_call_target="tpu_custom_call" | custom-call | tf_op jit(solution)/shard_map/pallas_call | solution.py:398
  179.0 2.9 convolution_convert_fusion.6
  183.3 12.6 %shard_map.181 = (bf16[3,1024,64]{2,1,0:T(8,128)(2,1)S(1)}, bf16[3,1024,64]{2,1,0:T(8,128)(2,1)S(1)}, bf16[3,1024,64]{2,1,0:T(8,128)(2,1)S(1)}) custom-call(bf16[3,1024,64]{2,1,0:T(8,128)(2,1)S(1)} %get-tuple-element.112.q_ref, bf16[3,1024,64]{2,1,0:T(8,128)(2,1)S(1)} %bitcast.117, f32[3,1024,1]{2,1,0:T(8,128)} %get-tuple-element.76.log_ref, ...), custom_call_target="tpu_custom_call" | custom-call | tf_op jit(solution)/shard_map/pallas_call | solution.py:564
  202.4 2.6 copy.36
  205.1 3.8 %convolution_convert_fusion.4 = bf16[4,2,96,576]{3,2,1,0:T(8,128)(2,1)} fusion(bf16[4,2,96,1024]{3,2,1,0:T(8,128)(2,1)} %bitcast.138, bf16[1024,192]{0,1:T(8,128)(2,1)S(1)} %bitcast.149, bf16[1024,192]{0,1:T(8,128)(2,1)S(1)} %bitcast.146, bf16[1024,192]{0,1:T(8,128)(2,1)S(1)} %bitcast.143), kind=kOutput, calls=%fused_computation.30 | convolution fusion | flops 909950976 | bytes 3637248 | tf_op jit(solution)/shard_map/dot_general | solution.py:670
  210.5 2.1 convolution_convert_fusion.5
  214.9 2.6 convolution_convert_fusion
  217.5 69.2 %shard_map.182 = (f32[256,768]{1,0:T(8,128)S(1)}, f32[96,768]{1,0:T(8,128)S(1)}, f32[96,1536]{1,0:T(8,128)S(1)}, f32[16,768]{1,0:T(8,128)S(1)}) custom-call(bf16[4,256,768]{2,1,0:T(8,128)(2,1)} %bitcast.142, bf16[256,768]{1,0:T(8,128)(2,1)S(1)} %copy-done.2, f32[256,768]{1,0:T(8,128)S(1)} %copy-done.10, f32[8,768]{1,0:T(8,128)S(1)} %copy-done.16, ...), custom_call_target="tpu_custom_call" | custom-call | tf_op jit(solution)/shard_map/pallas_call | solution.py:480
  (121 shorter events, 31.9 us)
Async XLA Ops:
  0.6 3.7 %copy-start.2 = (bf16[256,768]{1,0:T(8,128)(2,1)S(1)}, bf16[256,768]{1,0:T(8,128)(2,1)}, u32[]{:S(2)}) copy-start(bf16[256,768]{1,0:T(8,128)(2,1)} %x_ref.5) | copy-start | bytes 1179652
  0.7 3.7 %copy-start.3 = (bf16[256,768]{1,0:T(8,128)(2,1)S(1)}, bf16[256,768]{1,0:T(8,128)(2,1)}, u32[]{:S(2)}) copy-start(bf16[256,768]{1,0:T(8,128)(2,1)} %cot.1) | copy-start | bytes 1179652
  65.5 3.1 %copy-start.28 = (f32[8,16,128]{2,1,0:T(8,128)}, f32[8,16,128]{2,1,0:T(8,128)S(1)}, u32[]{:S(2)}) copy-start(f32[8,16,128]{2,1,0:T(8,128)S(1)} %dynamic-slice_bitcast_fusion) | copy-start | bytes 196612
  72.8 12.9 %copy-start = (bf16[3,1024,64]{2,1,0:T(8,128)(2,1)}, bf16[3,1024,64]{2,1,0:T(8,128)(2,1)S(1)}, u32[]{:S(2)}) copy-start(bf16[3,1024,64]{2,1,0:T(8,128)(2,1)S(1)} %get-tuple-element.110.v_ref) | copy-start | bytes 1179652
  72.8 12.9 %copy-start.1 = (bf16[3,1024,64]{2,1,0:T(8,128)(2,1)}, bf16[3,1024,64]{2,1,0:T(8,128)(2,1)S(1)}, u32[]{:S(2)}) copy-start(bf16[3,1024,64]{2,1,0:T(8,128)(2,1)S(1)} %get-tuple-element.111.k_ref) | copy-start | bytes 1179652
  85.7 3.2 %copy-start.21 = (bf16[1024,3,64]{0,2,1:T(8,128)(2,1)}, bf16[1024,3,64]{0,2,1:T(8,128)(2,1)S(1)}, u32[]{:S(2)}) copy-start(bf16[1024,3,64]{0,2,1:T(8,128)(2,1)S(1)} %copy.30) | copy-start | bytes 1179652
  85.7 3.1 %copy-start.27 = (f32[8,8,4,24]{3,0,2,1:T(8,128)S(1)}, f32[8,8,4,24]{3,0,2,1:T(8,128)}, u32[]{:S(2)}) copy-start(f32[8,8,4,24]{3,0,2,1:T(8,128)} %copy-done.26) | copy-start | bytes 73732
  89.0 55.6 %copy-start.15 = (f32[8,768]{1,0:T(8,128)}, f32[8,768]{1,0:T(8,128)S(1)}, u32[]{:S(2)}) copy-start(f32[8,768]{1,0:T(8,128)S(1)} %reshape.219.vec) | copy-start | bytes 73732
  117.2 4.2 %copy-start.19 = (bf16[4,256,768]{2,1,0:T(8,128)(2,1)S(1)}, bf16[4,256,768]{2,1,0:T(8,128)(2,1)}, u32[]{:S(2)}) copy-start(bf16[4,256,768]{2,1,0:T(8,128)(2,1)} %get-tuple-element.66) | copy-start | bytes 4718596
  117.2 4.2 %copy-start.29 = (bf16[4,2,96,1536]{3,2,1,0:T(8,128)(2,1)S(1)}, bf16[4,2,96,1536]{3,2,1,0:T(8,128)(2,1)}, u32[]{:S(2)}) copy-start(bf16[4,2,96,1536]{3,2,1,0:T(8,128)(2,1)} %get-tuple-element.67) | copy-start | bytes 7077892
  126.9 4.4 %copy-start.20 = (bf16[4,256,768]{2,1,0:T(8,128)(2,1)S(1)}, bf16[4,256,768]{2,1,0:T(8,128)(2,1)}, u32[]{:S(2)}) copy-start(bf16[4,256,768]{2,1,0:T(8,128)(2,1)} %get-tuple-element.66) | copy-start | bytes 4718596
  133.0 3.4 %copy-start.24 = (bf16[4,2,96,768]{3,2,1,0:T(8,128)(2,1)S(1)}, bf16[4,2,96,768]{3,2,1,0:T(8,128)(2,1)}, u32[]{:S(2)}) copy-start(bf16[4,2,96,768]{3,2,1,0:T(8,128)(2,1)} %fusion.14) | copy-start | bytes 3538948
  136.3 2.5 copy-start.30
  136.3 3.0 %copy-start.32 = (bf16[1024,768]{1,0:T(8,128)(2,1)S(1)}, bf16[1024,768]{1,0:T(8,128)(2,1)}, u32[]{:S(2)}) copy-start(bf16[1024,768]{1,0:T(8,128)(2,1)} %get-tuple-element.122) | copy-start | bytes 4718596
  139.3 2.7 copy-start.31
  142.0 2.6 copy-start.12
  179.0 2.9 copy-start.9
  179.0 2.9 copy-start.17
  198.5 2.9 copy-start.5
  202.4 2.6 copy-start.23
  212.6 2.3 copy-start.14
  214.8 2.6 copy-start.10
  214.9 2.6 copy-start.16
  286.6 5.2 %copy-start.18 = (bf16[256,768]{1,0:T(8,128)(2,1)S(1)}, bf16[256,768]{1,0:T(8,128)(2,1)}, u32[]{:S(2)}) copy-start(bf16[256,768]{1,0:T(8,128)(2,1)} %copy-done.17) | copy-start | bytes 1179652
  (9 other events, 11.4 us)
